TPU v7x, 32 devices: a whole 2x2x4 slice. The times are simulated.
32 devices in a mesh: tm: 8 (over z, core), ang: 2 (over x), ax: 2 (over y).
Axes of the slice: x: 2, y: 2, z: 4, core: 2. Of those that a mesh axis runs over, the one named last changes fastest.
Arguments:
- window_starts: float32 [8, 32, 32, 1152], P('tm', 'ang', 'ax'), may hold values from -6 to 6
- drive_source: float32 [8, 32, 32, 1152], P('tm', 'ang', 'ax'), may hold values from -6 to 6
- region_ids: int32 [32, 32, 1152], P('ang', 'ax'), may hold values from 0 to 7
- window_steps: int32 [8], replicated, may hold values from 1 to 4, as said below
- reluctivity: float32 [8], replicated, may hold values from 0.3 to 1
- resistivity: float32 [8], replicated, may hold values from 0.3 to 1
- relax_rates: float32 [8], replicated, may hold values from 0.02 to 0.14
Outputs:
- new_starts: float32 [8, 32, 32, 1152], P('tm', 'ang', 'ax')
Inputs may be any that keep to these rules, and one draw needn't show every extreme that they name: `window_steps`: every window takes 1 to 4 fine steps, and some window takes 4.
All inputs are finite; a program needn't handle non-finite values.
Results may differ from a plain program's by a relative error of at most 0.0003.
Values sent between devices are 32-bit elements; how exact they have to be, the bound alone decides.
A program may use at most 128 MiB of HBM per device.

v0:
```python
import functools

import jax
import jax.numpy as jnp
import ml_dtypes
import numpy as np
from jax import lax
from jax.experimental import pallas as pl
from jax.experimental.pallas import tpu as pltpu
from jax.sharding import PartitionSpec as P

STEPS = 4
LANES = 384
WIDE = 256
EDGE = 128
CHUNK = 128
AHEAD = 5
LAG = 5
GROUPS = (1, 2, 3, 4)

radial_weight = 1.0
explicit_limit = 0.23
F32 = jnp.float32
BF16 = jnp.bfloat16


def inverse_blocks(size):
    middle = 2.0 + 1.0 / radial_weight
    r = (middle - np.sqrt(middle * middle - 4.0)) / 2.0
    index = np.arange(size, dtype=np.float64)
    low = np.minimum(index[:, None], index[None, :])
    high = np.maximum(index[:, None], index[None, :])
    full = r ** (high - low) * (1 - r ** (2 * low + 2)) * (1 - r ** (2 * (size - high)))
    full = full / ((1 / r - r) * (1 - r ** (2 * size + 2)) * radial_weight)
    full = full.astype(np.float32)
    blocks, places, seen = [], [], {}
    for start in range(0, size, WIDE):
        stop = min(start + WIDE, size)
        first, last = max(start - EDGE, 0), min(stop + EDGE, size)
        block = np.ascontiguousarray(full[first:last, start:stop])
        key = (block.shape, block.tobytes())
        if key not in seen:
            seen[key] = len(blocks)
            top = block.astype(ml_dtypes.bfloat16)
            rest = (block - top.astype(np.float32)).astype(ml_dtypes.bfloat16)
            blocks.append((top, rest))
        places.append((start, stop, first, last, seen[key]))
    return blocks, places


def kernel(sizes, places, nblocks, *refs):
    tm_count, ang_count, ax_count = sizes
    steps_ref, reluct_ref, resist_ref, rates_ref, s_hbm, q_hbm, ids_hbm = refs[:7]
    w_hbm = refs[7 : 7 + 2 * nblocks]
    out_ref = refs[7 + 2 * nblocks]
    (
        q_ref, ids_ref, u, ca, cc, cb, rc, xh, xl, ha, hz, sa, sz,
        gs, off, dif, other, rdif, fs, fp, inv, fe, fo,
        pair, pin, sin, pout, sout, mine, give, got,
        a_send, a_recv, z_send, z_recv, o_send, o_recv,
        d_send, d_recv, p_send, p_recv, q_send, q_recv, c_send, c_recv, in_sem, *w_refs
    ) = refs[8 + 2 * nblocks :]
    na, nz, rad = u.shape
    half = na // 2
    part = half // 2
    regions = rates_ref.shape[0]
    tm, ang, ax = lax.axis_index("tm"), lax.axis_index("ang"), lax.axis_index("ax")
    core, chip = lax.rem(tm, 2), tm // 2
    chips = tm_count // 2
    mate = tm + 1 - 2 * core

    def ring(value, step, count):
        return lax.rem(value + step + count, count)

    loads = [(s_hbm.at[0], u), (ids_hbm, ids_ref), (q_hbm.at[0], q_ref), *zip(w_hbm, w_refs)]
    loads = [pltpu.make_async_copy(a, b, in_sem.at[n]) for n, (a, b) in enumerate(loads)]
    for load in loads:
        load.start()

    barrier = pltpu.get_barrier_semaphore()
    greet = [("ang", ang, 1, ang_count), ("ang", ang, -1, ang_count)]
    greet += [("ax", ax, 1, ax_count), ("ax", ax, -1, ax_count)]
    greet += [("tm", tm, step, tm_count) for step in (1, -1, 2, -2)]
    for axis, value, step, count in greet:
        pl.semaphore_signal(
            barrier, inc=1, device_id={axis: ring(value, step, count)},
            device_id_type=pl.DeviceIdType.MESH,
        )

    def remote(src, dst, send, recv, device):
        return pltpu.make_async_remote_copy(
            src_ref=src, dst_ref=dst, send_sem=send, recv_sem=recv,
            device_id=device, device_id_type=pl.DeviceIdType.MESH,
        )

    groups = [(places[a][0], places[b - 1][1]) for a, b in zip((0,) + GROUPS, GROUPS + (len(places),))]

    def ang_copy(t, block, side):
        lanes = slice(*groups[block])
        return remote(
            sa.at[t, side, :, lanes], ha.at[t, 1 - side, :, lanes],
            a_send.at[t, block, side], a_recv.at[t, block, 1 - side],
            {"ang": ring(ang, 2 * side - 1, ang_count)},
        )

    def ax_copy(t, block, side):
        lanes = slice(*groups[block])
        return remote(
            sz.at[t, side, :, lanes], hz.at[t, 1 - side, :, lanes],
            z_send.at[t, block, side], z_recv.at[t, block, 1 - side],
            {"ax": ring(ax, 2 * side - 1, ax_count)},
        )

    def pack(t, block):
        lanes = slice(*groups[block])
        sa[t, 0, :, lanes] = u[0, :, lanes]
        sa[t, 1, :, lanes] = u[na - 1, :, lanes]

        for a in range(na):
            sz[t, 0, a : a + 1, lanes] = u[a, 0:1, lanes]
            sz[t, 1, a : a + 1, lanes] = u[a, nz - 1 : nz, lanes]

    def send_halo(t, block):
        ang_copy(t, block, 0).start()
        ang_copy(t, block, 1).start()

        @pl.when(ax > 0)
        def _():
            ax_copy(t, block, 0).start()

        @pl.when(ax < ax_count - 1)
        def _():
            ax_copy(t, block, 1).start()

    def wait_halo(t, block):
        ang_copy(t, block, 0).wait()
        ang_copy(t, block, 1).wait()

        @pl.when(ax > 0)
        def _():
            ax_copy(t, block, 0).wait_send()
            ax_copy(t, block, 1).wait_recv()

        @pl.when(ax < ax_count - 1)
        def _():
            ax_copy(t, block, 1).wait_send()
            ax_copy(t, block, 0).wait_recv()

    @pl.when(ax == 0)
    def _():
        hz[:, 0] = jnp.zeros((STEPS, na, rad), F32)

    @pl.when(ax == ax_count - 1)
    def _():
        hz[:, 1] = jnp.zeros((STEPS, na, rad), F32)

    @pl.when(chip == 0)
    def _():
        pin[...] = jnp.zeros_like(pin)

    @pl.when(chip == chips - 1)
    def _():
        sin[...] = jnp.zeros_like(sin)

    loads[0].wait()
    for block in range(len(groups)):
        pack(0, block)
    pl.semaphore_wait(barrier, len(greet))
    for block in range(len(groups)):
        send_halo(0, block)

    loads[1].wait()
    loads[2].wait()
    reluct = [explicit_limit * reluct_ref[k] * resist_ref[k] for k in range(regions)]
    rates = [rates_ref[k] for k in range(regions)]
    own_steps = steps_ref[tm]

    def tables(a, _):
        for l in range(0, rad, LANES):
            cut = slice(l, l + LANES)
            ids = ids_ref[a, :, cut]
            coupling = jnp.zeros(ids.shape, F32)
            relax = jnp.zeros(ids.shape, F32)
            for k in range(regions):
                hit = ids == k
                coupling = jnp.where(hit, reluct[k], coupling)
                relax = jnp.where(hit, rates[k], relax)
            cc[a, :, cut] = coupling
            ca[a, :, cut] = 1.0 - 4.0 * coupling - relax
            cb[a, :, cut] = relax * q_ref[a, :, cut]
            previous = rc[a // 2, :, cut]
            rc[a // 2, :, cut] = jnp.where(lax.rem(a, 2) == 0, relax, 0.5 * (previous + relax))
        return 0

    lax.fori_loop(0, na, tables, 0)

    def own_factor(i, _):
        mean = (u[2 * i] + u[2 * i + 1]) * 0.5
        gs[i] = mean / (1.0 + own_steps.astype(F32) * rc[i])
        return 0

    lax.fori_loop(0, half, own_factor, 0)

    def factors(k, _):
        rate = rc[part * core + k]
        before = jnp.ones_like(rate)
        after = jnp.ones_like(rate)
        for j in range(tm_count):
            count = steps_ref[j].astype(F32)
            before = before * (1.0 + jnp.where(j < 2 * chip, count, 0.0) * rate)
            after = after * (1.0 + jnp.where(j > 2 * chip + 1, count, 0.0) * rate)
        even = 1.0 + steps_ref[2 * chip].astype(F32) * rate
        odd = 1.0 + steps_ref[2 * chip + 1].astype(F32) * rate
        whole = before * after * (even * odd)
        fs[k] = 1.0 / after
        fp[k] = 1.0 / before
        fe[k] = 1.0 / even
        fo[k] = 1.0 / odd
        inv[k] = whole / (whole - 1.0)
        return 0

    lax.fori_loop(0, part, factors, 0)
    for load in loads[3:]:
        load.wait()

    chunks = rad // CHUNK

    def lanes_of(k):
        return pl.ds(pl.multiple_of(k * CHUNK, CHUNK), CHUNK)

    ours, yours = pl.ds(part * core, part), pl.ds(part * (1 - core), part)

    def mate_copy(k):
        cut = lanes_of(k)
        return remote(
            off.at[yours, :, cut], other.at[:, :, cut], o_send.at[k], o_recv.at[k], {"tm": mate}
        )

    def change_copy(k):
        cut = lanes_of(k)
        return remote(
            dif.at[:, :, cut], rdif.at[:, :, cut], d_send.at[k], d_recv.at[k],
            {"tm": ring(tm, 1, tm_count)},
        )

    def forward_copy(k):
        cut = lanes_of(k)
        return remote(
            pout.at[:, :, cut], pin.at[:, :, cut], p_send.at[k], p_recv.at[k],
            {"tm": ring(tm, 2, tm_count)},
        )

    def backward_copy(k):
        cut = lanes_of(k)
        return remote(
            sout.at[:, :, cut], sin.at[:, :, cut], q_send.at[k], q_recv.at[k],
            {"tm": ring(tm, -2, tm_count)},
        )

    def coarse_copy(k):
        cut = lanes_of(k)
        return remote(
            give.at[:, :, cut], got.at[:, :, cut], c_send.at[k], c_recv.at[k], {"tm": mate}
        )

    def loop(body, first=0, last=chunks):
        def step(k, _):
            body(k)
            return 0

        lax.fori_loop(first, last, step, 0)

    def offsets(k):
        cut = lanes_of(k)
        for i in range(half):
            even, odd = u[2 * i, :, cut], u[2 * i + 1, :, cut]
            off[i, :, cut] = (even + odd) * 0.5 - gs[i, :, cut]
            dif[i, :, cut] = (even - odd) * 0.5
        mate_copy(k).start()

        @pl.when(core == 0)
        def _():
            change_copy(k).start()

    def fine(t, _):
        def moved(lanes, a, above, below):
            rows = pl.ds(pl.multiple_of(a * nz, nz), nz)
            cut = slice(*lanes)
            here = u[a, :, cut]
            spot = lax.broadcasted_iota(jnp.int32, here.shape, 0)
            left = jnp.where(spot == 0, hz[t, 0, pl.ds(a, 1), cut], pltpu.roll(here, 1, 0))
            right = jnp.where(
                spot == nz - 1, hz[t, 1, pl.ds(a, 1), cut], pltpu.roll(here, nz - 1, 0)
            )
            beside = (above + below) + (left + right)
            value = ca[a, :, cut] * here + cc[a, :, cut] * beside + cb[a, :, cut]
            top = value.astype(BF16)
            xh[rows, cut] = top
            xl[rows, cut] = (value - top.astype(F32)).astype(BF16)

        def stencil(lanes):
            cut = slice(*lanes)

            def inner(a, _):
                moved(lanes, a, u[a - 1, :, cut], u[a + 1, :, cut])
                return 0

            moved(lanes, 0, ha[t, 0, :, cut], u[1, :, cut])
            lax.fori_loop(1, na - 1, inner, 0)
            moved(lanes, na - 1, u[na - 2, :, cut], ha[t, 1, :, cut])

        ready, arrived = 0, 0
        for block, (start, stop, first, last, which) in enumerate(places):
            while arrived < len(groups) and groups[arrived][0] < last:
                wait_halo(t, arrived)
                arrived += 1
            if ready < last:
                stencil((ready, last))
                ready = last
            high, low = w_refs[2 * which], w_refs[2 * which + 1]
            left, rest = xh[:, first:last], xl[:, first:last]
            total = jnp.dot(left, high[...], preferred_element_type=F32)
            total += jnp.dot(rest, high[...], preferred_element_type=F32)
            total += jnp.dot(left, low[...], preferred_element_type=F32)
            total = total.reshape(na, nz, stop - start)
            active = jnp.full(total.shape, own_steps, jnp.int32) > t
            u[:, :, start:stop] = jnp.where(active, total, u[:, :, start:stop])

            for group, (_, end) in enumerate(groups):
                if end == stop:

                    @pl.when(t < STEPS - 1)
                    def _():
                        pack(t + 1, group)
                        send_halo(t + 1, group)

            @pl.when(t == STEPS - 1)
            def _():
                loop(offsets, start // CHUNK, stop // CHUNK)

        return 0

    lax.fori_loop(0, STEPS, fine, 0)

    ends = (chip == 0) | (chip == chips - 1)
    near_odd = jnp.logical_not(ends) & (core == 1)

    def pairs(k):
        mate_copy(k).wait()
        cut = lanes_of(k)
        own, theirs = off[ours, :, cut], other[:, :, cut]
        even = jnp.where(core == 0, own, theirs)
        odd = jnp.where(core == 0, theirs, own)
        pair[:, :, cut] = fo[:, :, cut] * even + odd

    def forward(k):
        cut = lanes_of(k)

        @pl.when(chip > 0)
        def _():
            forward_copy(k).wait_recv()

        pout[:, :, cut] = fe[:, :, cut] * fo[:, :, cut] * pin[:, :, cut] + pair[:, :, cut]

        @pl.when(chip < chips - 1)
        def _():
            forward_copy(k).start()

    def backward(k):
        cut = lanes_of(k)

        @pl.when(chip < chips - 1)
        def _():
            backward_copy(k).wait_recv()

        sout[:, :, cut] = fs[:, :, cut] * pair[:, :, cut] + sin[:, :, cut]

        @pl.when(chip > 0)
        def _():
            backward_copy(k).start()

    def settle(k):
        cut = lanes_of(k)
        own, theirs = off[ours, :, cut], other[:, :, cut]
        first = jnp.where(core == 0, own, theirs)
        even = (fp[:, :, cut] * sout[:, :, cut] + pin[:, :, cut]) * inv[:, :, cut]
        odd = fe[:, :, cut] * even + first
        mine[:, :, cut] = jnp.where(core == 0, even, odd)
        give[:, :, cut] = jnp.where(core == 0, odd, even)
        coarse_copy(k).start()

    def send_change(k):
        change_copy(k).start()

    @pl.when(near_odd)
    def _():
        loop(send_change, 0, AHEAD)

    def both(first, second):
        def one(k):
            pairs(k)

            @pl.when(near_odd & (k + AHEAD < chunks))
            def _():
                send_change(k + AHEAD)

            first(k)

        def two(k):
            second(k)
            settle(k)

        @pl.when(ends)
        def _():
            loop(one)

            @pl.when(core == 1)
            def _():
                loop(send_change)

            loop(two)

        @pl.when(jnp.logical_not(ends))
        def _():
            loop(one, 0, LAG)

            def step(k):
                one(k)
                two(k - LAG)

            loop(step, LAG, chunks)
            loop(two, chunks - LAG, chunks)

    @pl.when(chip < chips // 2)
    def _():
        both(forward, backward)

    @pl.when(chip >= chips // 2)
    def _():
        both(backward, forward)

    def finish(k):
        cut = lanes_of(k)
        coarse_copy(k).wait()
        change_copy(k).wait()

        @pl.when(chip < chips - 1)
        def _():
            forward_copy(k).wait_send()

        @pl.when(chip > 0)
        def _():
            backward_copy(k).wait_send()

        for r in range(part):
            for row, coarse in ((part * core + r, mine), (part * (1 - core) + r, got)):
                change = rdif[row, :, cut]
                out_ref[0, 2 * row, :, cut] = coarse[r, :, cut] + change
                out_ref[0, 2 * row + 1, :, cut] = coarse[r, :, cut] - change

    loop(finish)


def solution(mesh):
    sizes = tuple(mesh.shape[name] for name in ("tm", "ang", "ax"))

    def local(starts, drive, region_ids, steps, reluctivity, resistivity, rates):
        na, nz, rad = region_ids.shape
        half, part = na // 2, na // 4
        blocks, places = inverse_blocks(rad)
        weights = [jnp.asarray(piece) for block in blocks for piece in block]
        smem = pl.BlockSpec(memory_space=pltpu.SMEM)
        anywhere = pl.BlockSpec(memory_space=pltpu.HBM)
        vmem = pl.BlockSpec(memory_space=pltpu.VMEM)

        def field(*lead):
            return pltpu.VMEM(lead + (nz, rad), F32)

        halo = pltpu.VMEM((STEPS, 2, nz, rad), F32)
        axial = pltpu.VMEM((STEPS, 2, na, rad), F32)
        dma = pltpu.SemaphoreType.DMA
        scratch = [
            field(na), pltpu.VMEM((na, nz, rad), jnp.int32),
            field(na), field(na), field(na), field(na), field(half),
            pltpu.VMEM((na * nz, rad), BF16), pltpu.VMEM((na * nz, rad), BF16),
            halo, axial, halo, axial,
            field(half), field(half), field(half), field(part), field(half),
        ]
        scratch += [field(part)] * 5 + [field(part)] * 8
        scratch += [dma((STEPS, len(GROUPS) + 1, 2))] * 4 + [dma((rad // CHUNK,))] * 10
        scratch += [dma((3 + len(weights),))]
        scratch += [pltpu.VMEM(piece.shape, BF16) for piece in weights]
        return pl.pallas_call(
            functools.partial(kernel, sizes, places, len(blocks)),
            out_shape=jax.ShapeDtypeStruct(starts.shape, F32),
            in_specs=[smem] * 4 + [anywhere] * (3 + len(weights)),
            out_specs=vmem,
            scratch_shapes=scratch,
            compiler_params=pltpu.CompilerParams(
                collective_id=0, has_side_effects=True, vmem_limit_bytes=60 * 2**20
            ),
        )(steps, reluctivity, resistivity, rates, starts, drive, region_ids, *weights)

    cells = P("tm", "ang", "ax", None)
    placed = (cells, cells, P("ang", "ax", None), P(), P(), P(), P())
    return jax.shard_map(local, mesh=mesh, in_specs=placed, out_specs=cells, check_vma=False)
```

profile of v0, /device:TPU:0, one launch (start us, length us, event | category | flops | bytes accessed | tf_op | source)
XLA Modules:
  0.0 53.4 jit_solution(7503164568863889706)
XLA Ops:
  0.0 51.0 %shard_map.127 = f32[1,16,16,1152]{3,2,1,0:T(8,128)} custom-call(s32[8]{0:T(128)} %refs_0_.1, f32[8]{0:T(128)} %refs_1_.1, f32[8]{0:T(128)} %refs_2_.1, f32[8]{0:T(128)} %refs_3_.1, f32[1,16,16,1152]{3,2,1,0:T(8,128)} %refs_4_.1, f32[1,16,16,1152]{3,2,1,0:T(8,128)} %refs_5_.1, s32[16,16,1152]{2,1,0:T(8,128)} %refs_6_.1, ...), custom_call_target="tpu_custom_call" | custom-call | tf_op jit(solution)/shard_map/pallas_call | solution.py:493
  51.0 2.4 %copy.15 = f32[1,16,16,1152]{3,2,1,0:T(8,128)} copy(f32[1,16,16,1152]{3,2,1,0:T(8,128)} %shard_map.127) | data formatting | bytes 2359296
where the time goes:
time: 53.6 us; the launch traced here: 53.4 us
  Pallas kernels  51 us (95%)
  local copies, waits for them, and re-layouts  2.36 us (4%)
    pallas_call x1, Pallas kernels, local(): pl.pallas_call(functools.partial(kernel, sizes, places, len(blocks)), out...  51 us
    unnamed x1, local copies, waits for them, and re-layouts  2.36 us

commit v1 on v0

--- a/solution.py
+++ b/solution.py
@@ -14,6 +14,9 @@
 WIDE = 256
 EDGE = 128
 CHUNK = 128
+TALL = 8
+SPLIT = 2
+VMEM_LIMIT = 60 * 2**20
 AHEAD = 5
 LAG = 5
 GROUPS = (1, 2, 3, 4)
@@ -52,14 +55,14 @@
     tm_count, ang_count, ax_count = sizes
     steps_ref, reluct_ref, resist_ref, rates_ref, s_hbm, q_hbm, ids_hbm = refs[:7]
     w_hbm = refs[7 : 7 + 2 * nblocks]
-    out_ref = refs[7 + 2 * nblocks]
+    coarse_ref, rdif = refs[7 + 2 * nblocks : 9 + 2 * nblocks]
     (
         q_ref, ids_ref, u, ca, cc, cb, rc, xh, xl, ha, hz, sa, sz,
-        gs, off, dif, other, rdif, fs, fp, inv, fe, fo,
-        pair, pin, sin, pout, sout, mine, give, got,
+        gs, off, dif, other, fs, fp, inv, fe, fo,
+        pair, pin, sin, pout, sout, mine, give,
         a_send, a_recv, z_send, z_recv, o_send, o_recv,
-        d_send, d_recv, p_send, p_recv, q_send, q_recv, c_send, c_recv, in_sem, *w_refs
-    ) = refs[8 + 2 * nblocks :]
+        d_send, d_recv, p_send, p_recv, q_send, q_recv, c_send, c_recv, in_sem, out_sem, *w_refs
+    ) = refs[9 + 2 * nblocks :]
     na, nz, rad = u.shape
     half = na // 2
     part = half // 2
@@ -79,7 +82,7 @@
 
     barrier = pltpu.get_barrier_semaphore()
     greet = [("ang", ang, 1, ang_count), ("ang", ang, -1, ang_count)]
-    greet += [("ax", ax, 1, ax_count), ("ax", ax, -1, ax_count)]
+    greet += [("ax", ax, 1, ax_count)]
     greet += [("tm", tm, step, tm_count) for step in (1, -1, 2, -2)]
     for axis, value, step, count in greet:
         pl.semaphore_signal(
@@ -103,12 +106,11 @@
             {"ang": ring(ang, 2 * side - 1, ang_count)},
         )
 
-    def ax_copy(t, block, side):
+    def ax_copy(t, block):
         lanes = slice(*groups[block])
         return remote(
-            sz.at[t, side, :, lanes], hz.at[t, 1 - side, :, lanes],
-            z_send.at[t, block, side], z_recv.at[t, block, 1 - side],
-            {"ax": ring(ax, 2 * side - 1, ax_count)},
+            sz.at[t, :, lanes], hz.at[t, ax, :, lanes],
+            z_send.at[t, block], z_recv.at[t, block], {"ax": 1 - ax},
         )
 
     def pack(t, block):
@@ -117,42 +119,19 @@
         sa[t, 1, :, lanes] = u[na - 1, :, lanes]
 
         for a in range(na):
-            sz[t, 0, a : a + 1, lanes] = u[a, 0:1, lanes]
-            sz[t, 1, a : a + 1, lanes] = u[a, nz - 1 : nz, lanes]
+            sz[t, a : a + 1, lanes] = jnp.where(ax == 0, u[a, nz - 1 : nz, lanes], u[a, 0:1, lanes])
 
     def send_halo(t, block):
         ang_copy(t, block, 0).start()
         ang_copy(t, block, 1).start()
-
-        @pl.when(ax > 0)
-        def _():
-            ax_copy(t, block, 0).start()
-
-        @pl.when(ax < ax_count - 1)
-        def _():
-            ax_copy(t, block, 1).start()
+        ax_copy(t, block).start()
 
     def wait_halo(t, block):
         ang_copy(t, block, 0).wait()
         ang_copy(t, block, 1).wait()
-
-        @pl.when(ax > 0)
-        def _():
-            ax_copy(t, block, 0).wait_send()
-            ax_copy(t, block, 1).wait_recv()
-
-        @pl.when(ax < ax_count - 1)
-        def _():
-            ax_copy(t, block, 1).wait_send()
-            ax_copy(t, block, 0).wait_recv()
-
-    @pl.when(ax == 0)
-    def _():
-        hz[:, 0] = jnp.zeros((STEPS, na, rad), F32)
-
-    @pl.when(ax == ax_count - 1)
-    def _():
-        hz[:, 1] = jnp.zeros((STEPS, na, rad), F32)
+        ax_copy(t, block).wait()
+
+    hz[:, ax] = jnp.zeros((STEPS, na, rad), F32)
 
     @pl.when(chip == 0)
     def _():
@@ -260,8 +239,12 @@
     def coarse_copy(k):
         cut = lanes_of(k)
         return remote(
-            give.at[:, :, cut], got.at[:, :, cut], c_send.at[k], c_recv.at[k], {"tm": mate}
-        )
+            give.at[:, :, cut], coarse_ref.at[ours, :, cut], c_send.at[k], c_recv.at[k], {"tm": mate}
+        )
+
+    def keep_copy(k):
+        cut = lanes_of(k)
+        return pltpu.make_async_copy(mine.at[:, :, cut], coarse_ref.at[ours, :, cut], out_sem.at[k])
 
     def loop(body, first=0, last=chunks):
         def step(k, _):
@@ -283,31 +266,31 @@
             change_copy(k).start()
 
     def fine(t, _):
-        def moved(lanes, a, above, below):
-            rows = pl.ds(pl.multiple_of(a * nz, nz), nz)
-            cut = slice(*lanes)
-            here = u[a, :, cut]
-            spot = lax.broadcasted_iota(jnp.int32, here.shape, 0)
-            left = jnp.where(spot == 0, hz[t, 0, pl.ds(a, 1), cut], pltpu.roll(here, 1, 0))
-            right = jnp.where(
-                spot == nz - 1, hz[t, 1, pl.ds(a, 1), cut], pltpu.roll(here, nz - 1, 0)
-            )
-            beside = (above + below) + (left + right)
-            value = ca[a, :, cut] * here + cc[a, :, cut] * beside + cb[a, :, cut]
-            top = value.astype(BF16)
-            xh[rows, cut] = top
-            xl[rows, cut] = (value - top.astype(F32)).astype(BF16)
+        spot = lax.broadcasted_iota(jnp.int32, (TALL, CHUNK), 0)
+        low_edge, high_edge = spot == 0, spot == TALL - 1
 
         def stencil(lanes):
-            cut = slice(*lanes)
-
-            def inner(a, _):
-                moved(lanes, a, u[a - 1, :, cut], u[a + 1, :, cut])
-                return 0
-
-            moved(lanes, 0, ha[t, 0, :, cut], u[1, :, cut])
-            lax.fori_loop(1, na - 1, inner, 0)
-            moved(lanes, na - 1, u[na - 2, :, cut], ha[t, 1, :, cut])
+            for l in range(*lanes, CHUNK):
+                cut = slice(l, l + CHUNK)
+                above, here = ha[t, 0, :, cut], u[0, :, cut]
+                for a in range(na):
+                    below = u[a + 1, :, cut] if a < na - 1 else ha[t, 1, :, cut]
+                    pieces = [here[r : r + TALL] for r in range(0, nz, TALL)]
+                    down = [pltpu.roll(piece, 1, 0) for piece in pieces]
+                    up = [pltpu.roll(piece, TALL - 1, 0) for piece in pieces]
+                    down = [hz[t, 0, a : a + 1, cut]] + down
+                    up = up + [hz[t, 1, a : a + 1, cut]]
+                    beside = [
+                        jnp.where(low_edge, down[r], down[r + 1]) + jnp.where(high_edge, up[r + 1], up[r])
+                        for r in range(len(pieces))
+                    ]
+                    beside = jnp.concatenate(beside, 0) + (above + below)
+                    value = ca[a, :, cut] * here + cc[a, :, cut] * beside + cb[a, :, cut]
+                    top = value.astype(BF16)
+                    rows = slice(a * nz, (a + 1) * nz)
+                    xh[rows, cut] = top
+                    xl[rows, cut] = (value - top.astype(F32)).astype(BF16)
+                    above, here = here, below
 
         ready, arrived = 0, 0
         for block, (start, stop, first, last, which) in enumerate(places):
@@ -319,9 +302,9 @@
                 ready = last
             high, low = w_refs[2 * which], w_refs[2 * which + 1]
             left, rest = xh[:, first:last], xl[:, first:last]
-            total = jnp.dot(left, high[...], preferred_element_type=F32)
-            total += jnp.dot(rest, high[...], preferred_element_type=F32)
-            total += jnp.dot(left, low[...], preferred_element_type=F32)
+            fields = jnp.concatenate([left, rest, left], 1)
+            weights = jnp.concatenate([high[...], high[...], low[...]], 0)
+            total = jnp.dot(fields, weights, preferred_element_type=F32)
             total = total.reshape(na, nz, stop - start)
             active = jnp.full(total.shape, own_steps, jnp.int32) > t
             u[:, :, start:stop] = jnp.where(active, total, u[:, :, start:stop])
@@ -388,6 +371,7 @@
         mine[:, :, cut] = jnp.where(core == 0, even, odd)
         give[:, :, cut] = jnp.where(core == 0, odd, even)
         coarse_copy(k).start()
+        keep_copy(k).start()
 
     def send_change(k):
         change_copy(k).start()
@@ -440,7 +424,7 @@
         both(backward, forward)
 
     def finish(k):
-        cut = lanes_of(k)
+        keep_copy(k).wait()
         coarse_copy(k).wait()
         change_copy(k).wait()
 
@@ -452,13 +436,13 @@
         def _():
             backward_copy(k).wait_send()
 
-        for r in range(part):
-            for row, coarse in ((part * core + r, mine), (part * (1 - core) + r, got)):
-                change = rdif[row, :, cut]
-                out_ref[0, 2 * row, :, cut] = coarse[r, :, cut] + change
-                out_ref[0, 2 * row + 1, :, cut] = coarse[r, :, cut] - change
-
     loop(finish)
+
+
+def spread(coarse_ref, change_ref, out_ref):
+    for r in range(coarse_ref.shape[0]):
+        out_ref[0, 2 * r] = coarse_ref[r] + change_ref[r]
+        out_ref[0, 2 * r + 1] = coarse_ref[r] - change_ref[r]
 
 
 def solution(mesh):
@@ -471,35 +455,45 @@
         weights = [jnp.asarray(piece) for block in blocks for piece in block]
         smem = pl.BlockSpec(memory_space=pltpu.SMEM)
         anywhere = pl.BlockSpec(memory_space=pltpu.HBM)
-        vmem = pl.BlockSpec(memory_space=pltpu.VMEM)
 
         def field(*lead):
             return pltpu.VMEM(lead + (nz, rad), F32)
 
         halo = pltpu.VMEM((STEPS, 2, nz, rad), F32)
         axial = pltpu.VMEM((STEPS, 2, na, rad), F32)
+        face = pltpu.VMEM((STEPS, na, rad), F32)
         dma = pltpu.SemaphoreType.DMA
         scratch = [
             field(na), pltpu.VMEM((na, nz, rad), jnp.int32),
             field(na), field(na), field(na), field(na), field(half),
             pltpu.VMEM((na * nz, rad), BF16), pltpu.VMEM((na * nz, rad), BF16),
-            halo, axial, halo, axial,
-            field(half), field(half), field(half), field(part), field(half),
+            halo, axial, halo, face,
+            field(half), field(half), field(half), field(part),
         ]
-        scratch += [field(part)] * 5 + [field(part)] * 8
-        scratch += [dma((STEPS, len(GROUPS) + 1, 2))] * 4 + [dma((rad // CHUNK,))] * 10
-        scratch += [dma((3 + len(weights),))]
+        scratch += [field(part)] * 5 + [field(part)] * 7
+        scratch += [dma((STEPS, len(GROUPS) + 1, 2))] * 2 + [dma((STEPS, len(GROUPS) + 1))] * 2 + [dma((rad // CHUNK,))] * 10
+        scratch += [dma((3 + len(weights),)), dma((rad // CHUNK,))]
         scratch += [pltpu.VMEM(piece.shape, BF16) for piece in weights]
-        return pl.pallas_call(
+        pairs = jax.ShapeDtypeStruct((half, nz, rad), F32)
+        coarse, change = pl.pallas_call(
             functools.partial(kernel, sizes, places, len(blocks)),
-            out_shape=jax.ShapeDtypeStruct(starts.shape, F32),
+            out_shape=(pairs, pairs),
             in_specs=[smem] * 4 + [anywhere] * (3 + len(weights)),
-            out_specs=vmem,
+            out_specs=[pl.BlockSpec(memory_space=pl.ANY)] * 2,
             scratch_shapes=scratch,
             compiler_params=pltpu.CompilerParams(
-                collective_id=0, has_side_effects=True, vmem_limit_bytes=60 * 2**20
+                collective_id=0, has_side_effects=True, vmem_limit_bytes=VMEM_LIMIT
             ),
         )(steps, reluctivity, resistivity, rates, starts, drive, region_ids, *weights)
+        rows = half // SPLIT
+        narrow = pl.BlockSpec((rows, nz, rad), lambda i: (i, 0, 0))
+        return pl.pallas_call(
+            spread,
+            grid=(SPLIT,),
+            out_shape=jax.ShapeDtypeStruct(starts.shape, F32),
+            in_specs=[narrow] * 2,
+            out_specs=pl.BlockSpec((1, 2 * rows, nz, rad), lambda i: (0, i, 0, 0)),
+        )(coarse, change)
 
     cells = P("tm", "ang", "ax", None)
     placed = (cells, cells, P("ang", "ax", None), P(), P(), P(), P())

time: 53.6 us -> 50.5 us (0.942)
  local copies, waits for them, and re-layouts: 2.36 us -> 0 us
  Pallas kernels: 51 us -> 50.3 us
    pallas_call x1, Pallas kernels: 51 us -> 48.2 us  [local(): pl.pallas_call(functools.partial(kernel, sizes, places, len(blocks)), out...]
    unnamed x1 -> x0, local copies, waits for them, and re-layouts: 2.36 us -> none
    pallas_call x0 -> x1, Pallas kernels: none -> 2.11 us  [local(): pl.pallas_call(spread, grid=(SPLIT,), out_shape=jax.ShapeDtypeStruct(star...]
where the time goes in v1:
time: 50.5 us; the launch traced here: 50.3 us
  Pallas kernels  50.3 us (100%)
    pallas_call x1, Pallas kernels, local(): pl.pallas_call(functools.partial(kernel, sizes, places, len(blocks)), out...  48.2 us
    pallas_call x1, Pallas kernels, local(): pl.pallas_call(spread, grid=(SPLIT,), out_shape=jax.ShapeDtypeStruct(star...  2.11 us

profile of v1, /device:TPU:0, one launch (start us, length us, event | category | flops | bytes accessed | tf_op | source)
XLA Modules:
  0.0 50.3 jit_solution(1052698527980102226)
XLA Ops:
  0.0 48.2 %shard_map.127 = (f32[8,16,1152]{2,1,0:T(8,128)}, f32[8,16,1152]{2,1,0:T(8,128)}) custom-call(s32[8]{0:T(128)} %refs_0_.1, f32[8]{0:T(128)} %refs_1_.1, f32[8]{0:T(128)} %refs_2_.1, f32[8]{0:T(128)} %refs_3_.1, f32[1,16,16,1152]{3,2,1,0:T(8,128)} %refs_4_.1, f32[1,16,16,1152]{3,2,1,0:T(8,128)} %refs_5_.1, s32[16,16,1152]{2,1,0:T(8,128)} %refs_6_.1, ...), custom_call_target="tpu_custom_call" | custom-call | tf_op jit(solution)/shard_map/pallas_call | solution.py:478
  48.2 2.1 %shard_map.128 = f32[1,16,16,1152]{3,2,1,0:T(8,128)} custom-call(f32[8,16,1152]{2,1,0:T(8,128)} %get-tuple-element.7.coarse_ref, f32[8,16,1152]{2,1,0:T(8,128)} %get-tuple-element.8.change_ref), custom_call_target="tpu_custom_call" | custom-call | tf_op jit(solution)/shard_map/pallas_call | solution.py:490

commit v2 on v1

--- a/solution.py
+++ b/solution.py
@@ -57,13 +57,13 @@
     w_hbm = refs[7 : 7 + 2 * nblocks]
     coarse_ref, rdif = refs[7 + 2 * nblocks : 9 + 2 * nblocks]
     (
-        q_ref, ids_ref, u, ca, cc, cb, rc, xh, xl, ha, hz, sa, sz,
+        q_ref, ids_ref, u, ca, cc, cb, rc, xh, xl, bh, bl, ha, hz, sz, inner, fa, fc, fb,
         gs, off, dif, other, fs, fp, inv, fe, fo,
         pair, pin, sin, pout, sout, mine, give,
         a_send, a_recv, z_send, z_recv, o_send, o_recv,
         d_send, d_recv, p_send, p_recv, q_send, q_recv, c_send, c_recv, in_sem, out_sem, *w_refs
     ) = refs[9 + 2 * nblocks :]
-    na, nz, rad = u.shape
+    na, nz, rad = ids_ref.shape
     half = na // 2
     part = half // 2
     regions = rates_ref.shape[0]
@@ -75,7 +75,7 @@
     def ring(value, step, count):
         return lax.rem(value + step + count, count)
 
-    loads = [(s_hbm.at[0], u), (ids_hbm, ids_ref), (q_hbm.at[0], q_ref), *zip(w_hbm, w_refs)]
+    loads = [(s_hbm.at[0], u.at[0]), (ids_hbm, ids_ref), (q_hbm.at[0], q_ref), *zip(w_hbm, w_refs)]
     loads = [pltpu.make_async_copy(a, b, in_sem.at[n]) for n, (a, b) in enumerate(loads)]
     for load in loads:
         load.start()
@@ -101,7 +101,7 @@
     def ang_copy(t, block, side):
         lanes = slice(*groups[block])
         return remote(
-            sa.at[t, side, :, lanes], ha.at[t, 1 - side, :, lanes],
+            u.at[lax.rem(t, 2), (na - 1) * side, :, lanes], ha.at[t, 1 - side, :, lanes],
             a_send.at[t, block, side], a_recv.at[t, block, 1 - side],
             {"ang": ring(ang, 2 * side - 1, ang_count)},
         )
@@ -109,17 +109,9 @@
     def ax_copy(t, block):
         lanes = slice(*groups[block])
         return remote(
-            sz.at[t, :, lanes], hz.at[t, ax, :, lanes],
+            sz.at[t, :, lanes], hz.at[t, :, lanes],
             z_send.at[t, block], z_recv.at[t, block], {"ax": 1 - ax},
         )
-
-    def pack(t, block):
-        lanes = slice(*groups[block])
-        sa[t, 0, :, lanes] = u[0, :, lanes]
-        sa[t, 1, :, lanes] = u[na - 1, :, lanes]
-
-        for a in range(na):
-            sz[t, a : a + 1, lanes] = jnp.where(ax == 0, u[a, nz - 1 : nz, lanes], u[a, 0:1, lanes])
 
     def send_halo(t, block):
         ang_copy(t, block, 0).start()
@@ -131,7 +123,18 @@
         ang_copy(t, block, 1).wait()
         ax_copy(t, block).wait()
 
-    hz[:, ax] = jnp.zeros((STEPS, na, rad), F32)
+    def by_side(body):
+        @pl.when(ax == 0)
+        def _():
+            body(nz - 1, nz - 2)
+
+        @pl.when(ax == 1)
+        def _():
+            body(0, 1)
+
+    def gather(field, face, into):
+        for a in range(na):
+            into[a : a + 1, :] = field[a, face : face + 1, :]
 
     @pl.when(chip == 0)
     def _():
@@ -142,8 +145,7 @@
         sin[...] = jnp.zeros_like(sin)
 
     loads[0].wait()
-    for block in range(len(groups)):
-        pack(0, block)
+    by_side(lambda face, near: gather(u.at[0], face, sz.at[0]))
     pl.semaphore_wait(barrier, len(greet))
     for block in range(len(groups)):
         send_halo(0, block)
@@ -173,8 +175,14 @@
 
     lax.fori_loop(0, na, tables, 0)
 
+    def side_tables(face, near):
+        for field, into in ((ca, fa), (cc, fc), (cb, fb)):
+            gather(field, face, into)
+
+    by_side(side_tables)
+
     def own_factor(i, _):
-        mean = (u[2 * i] + u[2 * i + 1]) * 0.5
+        mean = (u[0, 2 * i] + u[0, 2 * i + 1]) * 0.5
         gs[i] = mean / (1.0 + own_steps.astype(F32) * rc[i])
         return 0
 
@@ -256,7 +264,7 @@
     def offsets(k):
         cut = lanes_of(k)
         for i in range(half):
-            even, odd = u[2 * i, :, cut], u[2 * i + 1, :, cut]
+            even, odd = u[STEPS % 2, 2 * i, :, cut], u[STEPS % 2, 2 * i + 1, :, cut]
             off[i, :, cut] = (even + odd) * 0.5 - gs[i, :, cut]
             dif[i, :, cut] = (even - odd) * 0.5
         mate_copy(k).start()
@@ -265,62 +273,110 @@
         def _():
             change_copy(k).start()
 
-    def fine(t, _):
-        spot = lax.broadcasted_iota(jnp.int32, (TALL, CHUNK), 0)
-        low_edge, high_edge = spot == 0, spot == TALL - 1
-
-        def stencil(lanes):
-            for l in range(*lanes, CHUNK):
-                cut = slice(l, l + CHUNK)
-                above, here = ha[t, 0, :, cut], u[0, :, cut]
-                for a in range(na):
-                    below = u[a + 1, :, cut] if a < na - 1 else ha[t, 1, :, cut]
-                    pieces = [here[r : r + TALL] for r in range(0, nz, TALL)]
-                    down = [pltpu.roll(piece, 1, 0) for piece in pieces]
-                    up = [pltpu.roll(piece, TALL - 1, 0) for piece in pieces]
-                    down = [hz[t, 0, a : a + 1, cut]] + down
-                    up = up + [hz[t, 1, a : a + 1, cut]]
-                    beside = [
-                        jnp.where(low_edge, down[r], down[r + 1]) + jnp.where(high_edge, up[r + 1], up[r])
-                        for r in range(len(pieces))
-                    ]
-                    beside = jnp.concatenate(beside, 0) + (above + below)
-                    value = ca[a, :, cut] * here + cc[a, :, cut] * beside + cb[a, :, cut]
-                    top = value.astype(BF16)
-                    rows = slice(a * nz, (a + 1) * nz)
-                    xh[rows, cut] = top
-                    xl[rows, cut] = (value - top.astype(F32)).astype(BF16)
-                    above, here = here, below
+    spot = lax.broadcasted_iota(jnp.int32, (TALL, CHUNK), 0)
+    low_edge, high_edge = spot == 0, spot == TALL - 1
+
+    def shifted(here, before, after):
+        pieces = [here[r : r + TALL] for r in range(0, here.shape[0], TALL)]
+        down = [before] + [pltpu.roll(piece, 1, 0) for piece in pieces]
+        up = [pltpu.roll(piece, TALL - 1, 0) for piece in pieces] + [after]
+        both = [
+            jnp.where(low_edge, down[r], down[r + 1]) + jnp.where(high_edge, up[r + 1], up[r])
+            for r in range(len(pieces))
+        ]
+        return jnp.concatenate(both, 0)
+
+    def split(value, rows, cut, high, low):
+        top = value.astype(BF16)
+        high[rows, cut] = top
+        low[rows, cut] = (value - top.astype(F32)).astype(BF16)
+
+    def solve(place, high, low):
+        _, _, first, last, which = place
+        top, rest = w_refs[2 * which][...], w_refs[2 * which + 1][...]
+        left = high[:, first:last]
+        fields = jnp.concatenate([left, low[:, first:last], left], 1)
+        return jnp.dot(fields, jnp.concatenate([top, top, rest], 0), preferred_element_type=F32)
+
+    def inside(t, now, later):
+        def stencil(cut):
+            above, here = u[now, 0, :, cut], u[now, 1, :, cut]
+            for a in range(1, na - 1):
+                below = u[now, a + 1, :, cut]
+                beside = shifted(here, 0.0, 0.0) + (above + below)
+                value = ca[a, :, cut] * here + cc[a, :, cut] * beside + cb[a, :, cut]
+                split(value, slice((a - 1) * nz, a * nz), cut, xh, xl)
+                above, here = here, below
+
+        ready = 0
+        for place in places:
+            start, stop, _, last, _ = place
+            for l in range(ready, last, CHUNK):
+                stencil(slice(l, l + CHUNK))
+            ready = max(ready, last)
+            total = solve(place, xh, xl).reshape(na - 2, nz, stop - start)
+            active = jnp.full(total.shape, own_steps, jnp.int32) > t
+            u[later, 1 : na - 1, :, start:stop] = jnp.where(active, total, u[now, 1 : na - 1, :, start:stop])
+
+    def border(t, now, later):
+        def stencil(cut):
+            for n, a, above, below in (
+                (0, 0, ha[t, 0, :, cut], u[now, 1, :, cut]),
+                (1, na - 1, u[now, na - 2, :, cut], ha[t, 1, :, cut]),
+            ):
+                here = u[now, a, :, cut]
+                outer = hz[t, a : a + 1, cut]
+                before, after = jnp.where(ax == 0, 0.0, outer), jnp.where(ax == 0, outer, 0.0)
+                beside = shifted(here, before, after) + (above + below)
+                value = ca[a, :, cut] * here + cc[a, :, cut] * beside + cb[a, :, cut]
+                split(value, slice(n * nz, (n + 1) * nz), cut, bh, bl)
+            before, after = (
+                jnp.where(ax == 0, ha[t, side, nz - 1 : nz, cut], ha[t, side, 0:1, cut]) for side in (0, 1)
+            )
+            here = sz[t, :, cut]
+            beside = shifted(here, before, after) + (inner[:, cut] + hz[t, :, cut])
+            value = fa[:, cut] * here + fc[:, cut] * beside + fb[:, cut]
+            split(value, slice(2 * nz, 2 * nz + na), cut, bh, bl)
 
         ready, arrived = 0, 0
-        for block, (start, stop, first, last, which) in enumerate(places):
+        for place in places:
+            start, stop, _, last, _ = place
+            cut = slice(start, stop)
             while arrived < len(groups) and groups[arrived][0] < last:
                 wait_halo(t, arrived)
                 arrived += 1
-            if ready < last:
-                stencil((ready, last))
-                ready = last
-            high, low = w_refs[2 * which], w_refs[2 * which + 1]
-            left, rest = xh[:, first:last], xl[:, first:last]
-            fields = jnp.concatenate([left, rest, left], 1)
-            weights = jnp.concatenate([high[...], high[...], low[...]], 0)
-            total = jnp.dot(fields, weights, preferred_element_type=F32)
-            total = total.reshape(na, nz, stop - start)
-            active = jnp.full(total.shape, own_steps, jnp.int32) > t
-            u[:, :, start:stop] = jnp.where(active, total, u[:, :, start:stop])
+            for l in range(ready, last, CHUNK):
+                stencil(slice(l, l + CHUNK))
+            ready = max(ready, last)
+            total = solve(place, bh, bl)
+            old = jnp.concatenate([u[now, 0, :, cut], u[now, na - 1, :, cut], sz[t, :, cut]], 0)
+            total = jnp.where(jnp.full(total.shape, own_steps, jnp.int32) > t, total, old)
+            u[later, 0, :, cut] = total[:nz]
+            u[later, na - 1, :, cut] = total[nz : 2 * nz]
+            sz[t + 1, :, cut] = total[2 * nz :]
 
             for group, (_, end) in enumerate(groups):
                 if end == stop:
 
                     @pl.when(t < STEPS - 1)
                     def _():
-                        pack(t + 1, group)
                         send_halo(t + 1, group)
+
+            def scatter(face, near):
+                for a in range(1, na - 1):
+                    u[later, a, face : face + 1, cut] = sz[t + 1, a : a + 1, cut]
+
+            by_side(scatter)
 
             @pl.when(t == STEPS - 1)
             def _():
                 loop(offsets, start // CHUNK, stop // CHUNK)
 
+    def fine(t, _):
+        now, later = lax.rem(t, 2), lax.rem(t + 1, 2)
+        inside(t, now, later)
+        by_side(lambda face, near: gather(u.at[now], near, inner))
+        border(t, now, later)
         return 0
 
     lax.fori_loop(0, STEPS, fine, 0)
@@ -460,14 +516,16 @@
             return pltpu.VMEM(lead + (nz, rad), F32)
 
         halo = pltpu.VMEM((STEPS, 2, nz, rad), F32)
-        axial = pltpu.VMEM((STEPS, 2, na, rad), F32)
         face = pltpu.VMEM((STEPS, na, rad), F32)
         dma = pltpu.SemaphoreType.DMA
+        edge = pltpu.VMEM((na, rad), F32)
+        inside = pltpu.VMEM(((na - 2) * nz, rad), BF16)
+        border = pltpu.VMEM((2 * nz + na, rad), BF16)
         scratch = [
             field(na), pltpu.VMEM((na, nz, rad), jnp.int32),
-            field(na), field(na), field(na), field(na), field(half),
-            pltpu.VMEM((na * nz, rad), BF16), pltpu.VMEM((na * nz, rad), BF16),
-            halo, axial, halo, face,
+            field(2, na), field(na), field(na), field(na), field(half),
+            inside, inside, border, border,
+            halo, face, pltpu.VMEM((STEPS + 1, na, rad), F32), edge, edge, edge, edge,
             field(half), field(half), field(half), field(part),
         ]
         scratch += [field(part)] * 5 + [field(part)] * 7

time: 50.5 us -> 48.7 us (0.964)
  Pallas kernels: 50.3 us -> 48.5 us
    pallas_call x1, Pallas kernels: 48.2 us -> 46.4 us  [local(): pl.pallas_call(functools.partial(kernel, sizes, places, len(blocks)), out...]
where the time goes in v2:
time: 48.7 us; the launch traced here: 48.6 us
  Pallas kernels  48.5 us (100%)
    pallas_call x1, Pallas kernels, local(): pl.pallas_call(functools.partial(kernel, sizes, places, len(blocks)), out...  46.4 us
    pallas_call x1, Pallas kernels, local(): pl.pallas_call(spread, grid=(SPLIT,), out_shape=jax.ShapeDtypeStruct(star...  2.11 us

profile of v2, /device:TPU:0, one launch (start us, length us, event | category | flops | bytes accessed | tf_op | source)
XLA Modules:
  0.0 48.6 jit_solution(8668269675007857529)
XLA Ops:
  0.0 46.4 %shard_map.127 = (f32[8,16,1152]{2,1,0:T(8,128)}, f32[8,16,1152]{2,1,0:T(8,128)}) custom-call(s32[8]{0:T(128)} %refs_0_.1, f32[8]{0:T(128)} %refs_1_.1, f32[8]{0:T(128)} %refs_2_.1, f32[8]{0:T(128)} %refs_3_.1, f32[1,16,16,1152]{3,2,1,0:T(8,128)} %refs_4_.1, f32[1,16,16,1152]{3,2,1,0:T(8,128)} %refs_5_.1, s32[16,16,1152]{2,1,0:T(8,128)} %refs_6_.1, ...), custom_call_target="tpu_custom_call" | custom-call | tf_op jit(solution)/shard_map/pallas_call | solution.py:536
  46.4 2.1 %shard_map.128 = f32[1,16,16,1152]{3,2,1,0:T(8,128)} custom-call(f32[8,16,1152]{2,1,0:T(8,128)} %get-tuple-element.7.coarse_ref, f32[8,16,1152]{2,1,0:T(8,128)} %get-tuple-element.8.change_ref), custom_call_target="tpu_custom_call" | custom-call | tf_op jit(solution)/shard_map/pallas_call | solution.py:548

commit v3 on v2

--- a/solution.py
+++ b/solution.py
@@ -19,6 +19,8 @@
 VMEM_LIMIT = 60 * 2**20
 AHEAD = 5
 LAG = 5
+BURST = 6
+RATE = (1, 2)
 GROUPS = (1, 2, 3, 4)
 
 radial_weight = 1.0
@@ -261,6 +263,13 @@
 
         lax.fori_loop(first, last, step, 0)
 
+    ends = (chip == 0) | (chip == chips - 1)
+    near_odd = jnp.logical_not(ends) & (core == 1)
+    last_odd = (chip == chips - 1) & (core == 1)
+
+    def due(k):
+        return jnp.minimum(BURST + k * RATE[0] // RATE[1], chunks)
+
     def offsets(k):
         cut = lanes_of(k)
         for i in range(half):
@@ -269,7 +278,9 @@
             dif[i, :, cut] = (even - odd) * 0.5
         mate_copy(k).start()
 
-        @pl.when(core == 0)
+        soon = (core == 0) | (near_odd & (k < AHEAD)) | (last_odd & (k < BURST))
+
+        @pl.when(soon)
         def _():
             change_copy(k).start()
 
@@ -381,9 +392,6 @@
 
     lax.fori_loop(0, STEPS, fine, 0)
 
-    ends = (chip == 0) | (chip == chips - 1)
-    near_odd = jnp.logical_not(ends) & (core == 1)
-
     def pairs(k):
         mate_copy(k).wait()
         cut = lanes_of(k)
@@ -432,10 +440,6 @@
     def send_change(k):
         change_copy(k).start()
 
-    @pl.when(near_odd)
-    def _():
-        loop(send_change, 0, AHEAD)
-
     def both(first, second):
         def one(k):
             pairs(k)
@@ -446,6 +450,10 @@
 
             first(k)
 
+            @pl.when(last_odd)
+            def _():
+                loop(send_change, due(k), due(k + 1))
+
         def two(k):
             second(k)
             settle(k)
@@ -454,9 +462,13 @@
         def _():
             loop(one)
 
-            @pl.when(core == 1)
+            @pl.when((chip == 0) & (core == 1))
             def _():
                 loop(send_change)
+
+            @pl.when(last_odd)
+            def _():
+                loop(send_change, due(chunks), chunks)
 
             loop(two)
 

time: 48.7 us -> 45.1 us (0.926)
  Pallas kernels: 48.5 us -> 44.9 us
    pallas_call x1, Pallas kernels: 46.4 us -> 42.8 us  [local(): pl.pallas_call(functools.partial(kernel, sizes, places, len(blocks)), out...]
where the time goes in v3:
time: 45.1 us; the launch traced here: 44.9 us
  Pallas kernels  44.9 us (100%)
    pallas_call x1, Pallas kernels, local(): pl.pallas_call(functools.partial(kernel, sizes, places, len(blocks)), out...  42.8 us
    pallas_call x1, Pallas kernels, local(): pl.pallas_call(spread, grid=(SPLIT,), out_shape=jax.ShapeDtypeStruct(star...  2.11 us

profile of v3, /device:TPU:0, one launch (start us, length us, event | category | flops | bytes accessed | tf_op | source)
XLA Modules:
  0.0 44.9 jit_solution(2352935289412439441)
XLA Ops:
  0.0 42.8 %shard_map.127 = (f32[8,16,1152]{2,1,0:T(8,128)}, f32[8,16,1152]{2,1,0:T(8,128)}) custom-call(s32[8]{0:T(128)} %refs_0_.1, f32[8]{0:T(128)} %refs_1_.1, f32[8]{0:T(128)} %refs_2_.1, f32[8]{0:T(128)} %refs_3_.1, f32[1,16,16,1152]{3,2,1,0:T(8,128)} %refs_4_.1, f32[1,16,16,1152]{3,2,1,0:T(8,128)} %refs_5_.1, s32[16,16,1152]{2,1,0:T(8,128)} %refs_6_.1, ...), custom_call_target="tpu_custom_call" | custom-call | tf_op jit(solution)/shard_map/pallas_call | solution.py:548
  42.8 2.1 %shard_map.128 = f32[1,16,16,1152]{3,2,1,0:T(8,128)} custom-call(f32[8,16,1152]{2,1,0:T(8,128)} %get-tuple-element.7.coarse_ref, f32[8,16,1152]{2,1,0:T(8,128)} %get-tuple-element.8.change_ref), custom_call_target="tpu_custom_call" | custom-call | tf_op jit(solution)/shard_map/pallas_call | solution.py:560

commit v4 on v3

--- a/solution.py
+++ b/solution.py
@@ -21,7 +21,7 @@
 LAG = 5
 BURST = 6
 RATE = (1, 2)
-GROUPS = (1, 2, 3, 4)
+FRONT = ()
 
 radial_weight = 1.0
 explicit_limit = 0.23
@@ -39,8 +39,8 @@
     full = full / ((1 / r - r) * (1 - r ** (2 * size + 2)) * radial_weight)
     full = full.astype(np.float32)
     blocks, places, seen = [], [], {}
-    for start in range(0, size, WIDE):
-        stop = min(start + WIDE, size)
+    starts = [0, *range(size % WIDE or WIDE, size, WIDE)]
+    for start, stop in zip(starts, starts[1:] + [size]):
         first, last = max(start - EDGE, 0), min(stop + EDGE, size)
         block = np.ascontiguousarray(full[first:last, start:stop])
         key = (block.shape, block.tobytes())
@@ -53,13 +53,18 @@
     return blocks, places
 
 
+def send_groups(places):
+    cuts = sorted({0, *FRONT, *(stop for _, stop, *_ in places)})
+    return list(zip(cuts, cuts[1:]))
+
+
 def kernel(sizes, places, nblocks, *refs):
     tm_count, ang_count, ax_count = sizes
     steps_ref, reluct_ref, resist_ref, rates_ref, s_hbm, q_hbm, ids_hbm = refs[:7]
     w_hbm = refs[7 : 7 + 2 * nblocks]
     coarse_ref, rdif = refs[7 + 2 * nblocks : 9 + 2 * nblocks]
     (
-        q_ref, ids_ref, u, ca, cc, cb, rc, xh, xl, bh, bl, ha, hz, sz, inner, fa, fc, fb,
+        q_ref, ids_ref, u, ca, cc, cb, rc, xh, xl, bh, bl, ha, hz, sa, sz, inner, fa, fc, fb,
         gs, off, dif, other, fs, fp, inv, fe, fo,
         pair, pin, sin, pout, sout, mine, give,
         a_send, a_recv, z_send, z_recv, o_send, o_recv,
@@ -79,9 +84,6 @@
 
     loads = [(s_hbm.at[0], u.at[0]), (ids_hbm, ids_ref), (q_hbm.at[0], q_ref), *zip(w_hbm, w_refs)]
     loads = [pltpu.make_async_copy(a, b, in_sem.at[n]) for n, (a, b) in enumerate(loads)]
-    for load in loads:
-        load.start()
-
     barrier = pltpu.get_barrier_semaphore()
     greet = [("ang", ang, 1, ang_count), ("ang", ang, -1, ang_count)]
     greet += [("ax", ax, 1, ax_count)]
@@ -92,37 +94,46 @@
             device_id_type=pl.DeviceIdType.MESH,
         )
 
+    for load in loads:
+        load.start()
+
     def remote(src, dst, send, recv, device):
         return pltpu.make_async_remote_copy(
             src_ref=src, dst_ref=dst, send_sem=send, recv_sem=recv,
             device_id=device, device_id_type=pl.DeviceIdType.MESH,
         )
 
-    groups = [(places[a][0], places[b - 1][1]) for a, b in zip((0,) + GROUPS, GROUPS + (len(places),))]
-
-    def ang_copy(t, block, side):
+    groups = send_groups(places)
+
+    def ang_copies(t, block):
         lanes = slice(*groups[block])
-        return remote(
-            u.at[lax.rem(t, 2), (na - 1) * side, :, lanes], ha.at[t, 1 - side, :, lanes],
-            a_send.at[t, block, side], a_recv.at[t, block, 1 - side],
-            {"ang": ring(ang, 2 * side - 1, ang_count)},
-        )
+        if ang_count == 2:
+            routes = [(slice(None), 1 - ang)]
+        else:
+            routes = [(0, ring(ang, 1, ang_count)), (1, ring(ang, -1, ang_count))]
+        return [
+            remote(
+                sa.at[t, side, :, lanes], ha.at[t, side, :, lanes],
+                a_send.at[lax.rem(t, 2), block, n], a_recv.at[lax.rem(t, 2), block, n], {"ang": device},
+            )
+            for n, (side, device) in enumerate(routes)
+        ]
 
     def ax_copy(t, block):
         lanes = slice(*groups[block])
         return remote(
             sz.at[t, :, lanes], hz.at[t, :, lanes],
-            z_send.at[t, block], z_recv.at[t, block], {"ax": 1 - ax},
+            z_send.at[lax.rem(t, 2), block], z_recv.at[lax.rem(t, 2), block], {"ax": 1 - ax},
         )
 
     def send_halo(t, block):
-        ang_copy(t, block, 0).start()
-        ang_copy(t, block, 1).start()
+        for copy in ang_copies(t, block):
+            copy.start()
         ax_copy(t, block).start()
 
     def wait_halo(t, block):
-        ang_copy(t, block, 0).wait()
-        ang_copy(t, block, 1).wait()
+        for copy in ang_copies(t, block):
+            copy.wait()
         ax_copy(t, block).wait()
 
     def by_side(body):
@@ -147,6 +158,8 @@
         sin[...] = jnp.zeros_like(sin)
 
     loads[0].wait()
+    sa[0, 0] = u[0, na - 1]
+    sa[0, 1] = u[0, 0]
     by_side(lambda face, near: gather(u.at[0], face, sz.at[0]))
     pl.semaphore_wait(barrier, len(greet))
     for block in range(len(groups)):
@@ -215,6 +228,8 @@
     chunks = rad // CHUNK
 
     def lanes_of(k):
+        if k is None:
+            return slice(None)
         return pl.ds(pl.multiple_of(k * CHUNK, CHUNK), CHUNK)
 
     ours, yours = pl.ds(part * core, part), pl.ds(part * (1 - core), part)
@@ -222,39 +237,39 @@
     def mate_copy(k):
         cut = lanes_of(k)
         return remote(
-            off.at[yours, :, cut], other.at[:, :, cut], o_send.at[k], o_recv.at[k], {"tm": mate}
+            off.at[yours, :, cut], other.at[:, :, cut], o_send.at[0], o_recv.at[0 if k is None else k], {"tm": mate}
         )
 
     def change_copy(k):
         cut = lanes_of(k)
         return remote(
-            dif.at[:, :, cut], rdif.at[:, :, cut], d_send.at[k], d_recv.at[k],
+            dif.at[:, :, cut], rdif.at[:, :, cut], d_send.at[0], d_recv.at[0 if k is None else k],
             {"tm": ring(tm, 1, tm_count)},
         )
 
     def forward_copy(k):
         cut = lanes_of(k)
         return remote(
-            pout.at[:, :, cut], pin.at[:, :, cut], p_send.at[k], p_recv.at[k],
+            pout.at[:, :, cut], pin.at[:, :, cut], p_send.at[0], p_recv.at[0 if k is None else k],
             {"tm": ring(tm, 2, tm_count)},
         )
 
     def backward_copy(k):
         cut = lanes_of(k)
         return remote(
-            sout.at[:, :, cut], sin.at[:, :, cut], q_send.at[k], q_recv.at[k],
+            sout.at[:, :, cut], sin.at[:, :, cut], q_send.at[0], q_recv.at[0 if k is None else k],
             {"tm": ring(tm, -2, tm_count)},
         )
 
     def coarse_copy(k):
         cut = lanes_of(k)
         return remote(
-            give.at[:, :, cut], coarse_ref.at[ours, :, cut], c_send.at[k], c_recv.at[k], {"tm": mate}
+            give.at[:, :, cut], coarse_ref.at[ours, :, cut], c_send.at[0], c_recv.at[0 if k is None else k], {"tm": mate}
         )
 
     def keep_copy(k):
         cut = lanes_of(k)
-        return pltpu.make_async_copy(mine.at[:, :, cut], coarse_ref.at[ours, :, cut], out_sem.at[k])
+        return pltpu.make_async_copy(mine.at[:, :, cut], coarse_ref.at[ours, :, cut], out_sem.at[0])
 
     def loop(body, first=0, last=chunks):
         def step(k, _):
@@ -328,6 +343,10 @@
             total = solve(place, xh, xl).reshape(na - 2, nz, stop - start)
             active = jnp.full(total.shape, own_steps, jnp.int32) > t
             u[later, 1 : na - 1, :, start:stop] = jnp.where(active, total, u[now, 1 : na - 1, :, start:stop])
+
+    def scatter(t, later, cut, face, near):
+        for a in range(1, na - 1):
+            u[later, a, face : face + 1, cut] = sz[t + 1, a : a + 1, cut]
 
     def border(t, now, later):
         def stencil(cut):
@@ -364,36 +383,41 @@
             total = jnp.where(jnp.full(total.shape, own_steps, jnp.int32) > t, total, old)
             u[later, 0, :, cut] = total[:nz]
             u[later, na - 1, :, cut] = total[nz : 2 * nz]
+            sa[t + 1, 1, :, cut] = total[:nz]
+            sa[t + 1, 0, :, cut] = total[nz : 2 * nz]
             sz[t + 1, :, cut] = total[2 * nz :]
 
-            for group, (_, end) in enumerate(groups):
-                if end == stop:
-
-                    @pl.when(t < STEPS - 1)
-                    def _():
+            @pl.when(t < STEPS - 1)
+            def _():
+                for group, (begin, _) in enumerate(groups):
+                    if start <= begin < stop:
                         send_halo(t + 1, group)
-
-            def scatter(face, near):
-                for a in range(1, na - 1):
-                    u[later, a, face : face + 1, cut] = sz[t + 1, a : a + 1, cut]
-
-            by_side(scatter)
 
             @pl.when(t == STEPS - 1)
             def _():
+                by_side(functools.partial(scatter, t, later, cut))
                 loop(offsets, start // CHUNK, stop // CHUNK)
 
     def fine(t, _):
         now, later = lax.rem(t, 2), lax.rem(t + 1, 2)
         inside(t, now, later)
-        by_side(lambda face, near: gather(u.at[now], near, inner))
         border(t, now, later)
+
+        def ready(face, near):
+            scatter(t, later, slice(None), face, near)
+            gather(u.at[later], near, inner)
+
+        @pl.when(t < STEPS - 1)
+        def _():
+            by_side(ready)
+
         return 0
 
+    by_side(lambda face, near: gather(u.at[0], near, inner))
     lax.fori_loop(0, STEPS, fine, 0)
 
     def pairs(k):
-        mate_copy(k).wait()
+        mate_copy(k).wait_recv()
         cut = lanes_of(k)
         own, theirs = off[ours, :, cut], other[:, :, cut]
         even = jnp.where(core == 0, own, theirs)
@@ -443,17 +467,19 @@
     def both(first, second):
         def one(k):
             pairs(k)
+            first(k)
+
+            @pl.when(last_odd)
+            def _():
+                loop(send_change, due(k), due(k + 1))
+
+        def relay(k):
+            first(k)
 
             @pl.when(near_odd & (k + AHEAD < chunks))
             def _():
                 send_change(k + AHEAD)
 
-            first(k)
-
-            @pl.when(last_odd)
-            def _():
-                loop(send_change, due(k), due(k + 1))
-
         def two(k):
             second(k)
             settle(k)
@@ -474,10 +500,11 @@
 
         @pl.when(jnp.logical_not(ends))
         def _():
-            loop(one, 0, LAG)
+            loop(pairs)
+            loop(relay, 0, LAG)
 
             def step(k):
-                one(k)
+                relay(k)
                 two(k - LAG)
 
             loop(step, LAG, chunks)
@@ -492,19 +519,21 @@
         both(backward, forward)
 
     def finish(k):
-        keep_copy(k).wait()
-        coarse_copy(k).wait()
-        change_copy(k).wait()
-
-        @pl.when(chip < chips - 1)
-        def _():
-            forward_copy(k).wait_send()
-
-        @pl.when(chip > 0)
-        def _():
-            backward_copy(k).wait_send()
+        coarse_copy(k).wait_recv()
+        change_copy(k).wait_recv()
 
     loop(finish)
+    keep_copy(None).wait()
+    for copy in (mate_copy, coarse_copy, change_copy):
+        copy(None).wait_send()
+
+    @pl.when(chip < chips - 1)
+    def _():
+        forward_copy(None).wait_send()
+
+    @pl.when(chip > 0)
+    def _():
+        backward_copy(None).wait_send()
 
 
 def spread(coarse_ref, change_ref, out_ref):
@@ -537,12 +566,13 @@
             field(na), pltpu.VMEM((na, nz, rad), jnp.int32),
             field(2, na), field(na), field(na), field(na), field(half),
             inside, inside, border, border,
-            halo, face, pltpu.VMEM((STEPS + 1, na, rad), F32), edge, edge, edge, edge,
+            halo, face, pltpu.VMEM((STEPS + 1, 2, nz, rad), F32), pltpu.VMEM((STEPS + 1, na, rad), F32), edge, edge, edge, edge,
             field(half), field(half), field(half), field(part),
         ]
         scratch += [field(part)] * 5 + [field(part)] * 7
-        scratch += [dma((STEPS, len(GROUPS) + 1, 2))] * 2 + [dma((STEPS, len(GROUPS) + 1))] * 2 + [dma((rad // CHUNK,))] * 10
-        scratch += [dma((3 + len(weights),)), dma((rad // CHUNK,))]
+        count = len(send_groups(places))
+        scratch += [dma((2, count, 1 if sizes[1] == 2 else 2))] * 2 + [dma((2, count))] * 2 + [dma((1,)), dma((rad // CHUNK,))] * 5
+        scratch += [dma((3 + len(weights),)), dma((1,))]
         scratch += [pltpu.VMEM(piece.shape, BF16) for piece in weights]
         pairs = jax.ShapeDtypeStruct((half, nz, rad), F32)
         coarse, change = pl.pallas_call(

time: 45.1 us -> 43.7 us (0.969)
  Pallas kernels: 44.9 us -> 43.5 us
    pallas_call x1, Pallas kernels: 42.8 us -> 41.4 us  [local(): pl.pallas_call(functools.partial(kernel, sizes, places, len(blocks)), out...]
where the time goes in v4:
time: 43.7 us; the launch traced here: 43.5 us
  Pallas kernels  43.5 us (100%)
    pallas_call x1, Pallas kernels, local(): pl.pallas_call(functools.partial(kernel, sizes, places, len(blocks)), out...  41.4 us
    pallas_call x1, Pallas kernels, local(): pl.pallas_call(spread, grid=(SPLIT,), out_shape=jax.ShapeDtypeStruct(star...  2.11 us

profile of v4, /device:TPU:0, one launch (start us, length us, event | category | flops | bytes accessed | tf_op | source)
XLA Modules:
  0.0 43.5 jit_solution(17125744979874769509)
XLA Ops:
  0.0 41.4 %shard_map.127 = (f32[8,16,1152]{2,1,0:T(8,128)}, f32[8,16,1152]{2,1,0:T(8,128)}) custom-call(s32[8]{0:T(128)} %refs_0_.1, f32[8]{0:T(128)} %refs_1_.1, f32[8]{0:T(128)} %refs_2_.1, f32[8]{0:T(128)} %refs_3_.1, f32[1,16,16,1152]{3,2,1,0:T(8,128)} %refs_4_.1, f32[1,16,16,1152]{3,2,1,0:T(8,128)} %refs_5_.1, s32[16,16,1152]{2,1,0:T(8,128)} %refs_6_.1, ...), custom_call_target="tpu_custom_call" | custom-call | tf_op jit(solution)/shard_map/pallas_call | solution.py:578
  41.4 2.1 %shard_map.128 = f32[1,16,16,1152]{3,2,1,0:T(8,128)} custom-call(f32[8,16,1152]{2,1,0:T(8,128)} %get-tuple-element.7.coarse_ref, f32[8,16,1152]{2,1,0:T(8,128)} %get-tuple-element.8.change_ref), custom_call_target="tpu_custom_call" | custom-call | tf_op jit(solution)/shard_map/pallas_call | solution.py:590

commit v5 on v4

--- a/solution.py
+++ b/solution.py
@@ -58,19 +58,20 @@
     return list(zip(cuts, cuts[1:]))
 
 
-def kernel(sizes, places, nblocks, *refs):
+def kernel(sizes, places, depths, *refs):
+    nblocks = len(depths)
     tm_count, ang_count, ax_count = sizes
     steps_ref, reluct_ref, resist_ref, rates_ref, s_hbm, q_hbm, ids_hbm = refs[:7]
-    w_hbm = refs[7 : 7 + 2 * nblocks]
-    coarse_ref, rdif = refs[7 + 2 * nblocks : 9 + 2 * nblocks]
+    w_hbm, coarse_ref, rdif = refs[7:10]
     (
         q_ref, ids_ref, u, ca, cc, cb, rc, xh, xl, bh, bl, ha, hz, sa, sz, inner, fa, fc, fb,
         gs, off, dif, other, fs, fp, inv, fe, fo,
         pair, pin, sin, pout, sout, mine, give,
         a_send, a_recv, z_send, z_recv, o_send, o_recv,
-        d_send, d_recv, p_send, p_recv, q_send, q_recv, c_send, c_recv, in_sem, out_sem, *w_refs
-    ) = refs[9 + 2 * nblocks :]
+        d_send, d_recv, p_send, p_recv, q_send, q_recv, c_send, c_recv, in_sem, out_sem, w_all
+    ) = refs[10:]
     na, nz, rad = ids_ref.shape
+    wedges = dict(zip(range(nblocks), np.cumsum([0, *depths])))
     half = na // 2
     part = half // 2
     regions = rates_ref.shape[0]
@@ -82,7 +83,7 @@
     def ring(value, step, count):
         return lax.rem(value + step + count, count)
 
-    loads = [(s_hbm.at[0], u.at[0]), (ids_hbm, ids_ref), (q_hbm.at[0], q_ref), *zip(w_hbm, w_refs)]
+    loads = [(s_hbm.at[0], u.at[0]), (ids_hbm, ids_ref), (q_hbm.at[0], q_ref), (w_hbm, w_all)]
     loads = [pltpu.make_async_copy(a, b, in_sem.at[n]) for n, (a, b) in enumerate(loads)]
     barrier = pltpu.get_barrier_semaphore()
     greet = [("ang", ang, 1, ang_count), ("ang", ang, -1, ang_count)]
@@ -243,7 +244,7 @@
     def change_copy(k):
         cut = lanes_of(k)
         return remote(
-            dif.at[:, :, cut], rdif.at[:, :, cut], d_send.at[0], d_recv.at[0 if k is None else k],
+            dif.at[:, :, cut], rdif.at[:, :, cut], d_send.at[0], d_recv.at[0],
             {"tm": ring(tm, 1, tm_count)},
         )
 
@@ -264,7 +265,7 @@
     def coarse_copy(k):
         cut = lanes_of(k)
         return remote(
-            give.at[:, :, cut], coarse_ref.at[ours, :, cut], c_send.at[0], c_recv.at[0 if k is None else k], {"tm": mate}
+            give.at[:, :, cut], coarse_ref.at[ours, :, cut], c_send.at[0], c_recv.at[0], {"tm": mate}
         )
 
     def keep_copy(k):
@@ -318,8 +319,9 @@
         low[rows, cut] = (value - top.astype(F32)).astype(BF16)
 
     def solve(place, high, low):
-        _, _, first, last, which = place
-        top, rest = w_refs[2 * which][...], w_refs[2 * which + 1][...]
+        start, stop, first, last, which = place
+        row, deep, wide = 2 * wedges[which], last - first, stop - start
+        top, rest = w_all[row : row + deep, :wide], w_all[row + deep : row + 2 * deep, :wide]
         left = high[:, first:last]
         fields = jnp.concatenate([left, low[:, first:last], left], 1)
         return jnp.dot(fields, jnp.concatenate([top, top, rest], 0), preferred_element_type=F32)
@@ -518,14 +520,10 @@
     def _():
         both(backward, forward)
 
-    def finish(k):
-        coarse_copy(k).wait_recv()
-        change_copy(k).wait_recv()
-
-    loop(finish)
     keep_copy(None).wait()
-    for copy in (mate_copy, coarse_copy, change_copy):
-        copy(None).wait_send()
+    coarse_copy(None).wait()
+    change_copy(None).wait()
+    mate_copy(None).wait_send()
 
     @pl.when(chip < chips - 1)
     def _():
@@ -549,7 +547,9 @@
         na, nz, rad = region_ids.shape
         half, part = na // 2, na // 4
         blocks, places = inverse_blocks(rad)
-        weights = [jnp.asarray(piece) for block in blocks for piece in block]
+        weights = np.concatenate(
+            [np.pad(piece, ((0, 0), (0, WIDE - piece.shape[1]))) for block in blocks for piece in block]
+        )
         smem = pl.BlockSpec(memory_space=pltpu.SMEM)
         anywhere = pl.BlockSpec(memory_space=pltpu.HBM)
 
@@ -571,20 +571,21 @@
         ]
         scratch += [field(part)] * 5 + [field(part)] * 7
         count = len(send_groups(places))
-        scratch += [dma((2, count, 1 if sizes[1] == 2 else 2))] * 2 + [dma((2, count))] * 2 + [dma((1,)), dma((rad // CHUNK,))] * 5
-        scratch += [dma((3 + len(weights),)), dma((1,))]
-        scratch += [pltpu.VMEM(piece.shape, BF16) for piece in weights]
+        scratch += [dma((2, count, 1 if sizes[1] == 2 else 2))] * 2 + [dma((2, count))] * 2 + [dma((1,)), dma((rad // CHUNK,)), dma((1,)), dma((1,))]
+        scratch += [dma((1,)), dma((rad // CHUNK,))] * 2 + [dma((1,))] * 2
+        scratch += [dma((4,)), dma((1,))]
+        scratch += [pltpu.VMEM(weights.shape, BF16)]
         pairs = jax.ShapeDtypeStruct((half, nz, rad), F32)
         coarse, change = pl.pallas_call(
-            functools.partial(kernel, sizes, places, len(blocks)),
+            functools.partial(kernel, sizes, places, [top.shape[0] for top, _ in blocks]),
             out_shape=(pairs, pairs),
-            in_specs=[smem] * 4 + [anywhere] * (3 + len(weights)),
+            in_specs=[smem] * 4 + [anywhere] * 4,
             out_specs=[pl.BlockSpec(memory_space=pl.ANY)] * 2,
             scratch_shapes=scratch,
             compiler_params=pltpu.CompilerParams(
                 collective_id=0, has_side_effects=True, vmem_limit_bytes=VMEM_LIMIT
             ),
-        )(steps, reluctivity, resistivity, rates, starts, drive, region_ids, *weights)
+        )(steps, reluctivity, resistivity, rates, starts, drive, region_ids, jnp.asarray(weights))
         rows = half // SPLIT
         narrow = pl.BlockSpec((rows, nz, rad), lambda i: (i, 0, 0))
         return pl.pallas_call(

time: 43.7 us -> 43.5 us (level)
  no operation moved by 1% of the time
where the time goes in v5:
time: 43.5 us; the launch traced here: 43.3 us
  Pallas kernels  43.3 us (100%)
    pallas_call x1, Pallas kernels, local(): pl.pallas_call(functools.partial(kernel, sizes, places, [top.shape[0] for...  41.2 us
    pallas_call x1, Pallas kernels, local(): pl.pallas_call(spread, grid=(SPLIT,), out_shape=jax.ShapeDtypeStruct(star...  2.11 us

profile of v5, /device:TPU:0, one launch (start us, length us, event | category | flops | bytes accessed | tf_op | source)
XLA Modules:
  0.0 43.3 jit_solution(15001302555942775271)
XLA Ops:
  0.0 41.2 %shard_map.82 = (f32[8,16,1152]{2,1,0:T(8,128)}, f32[8,16,1152]{2,1,0:T(8,128)}) custom-call(s32[8]{0:T(128)} %refs_0_.1, f32[8]{0:T(128)} %refs_1_.1, f32[8]{0:T(128)} %refs_2_.1, f32[8]{0:T(128)} %refs_3_.1, f32[1,16,16,1152]{3,2,1,0:T(8,128)} %refs_4_.1, f32[1,16,16,1152]{3,2,1,0:T(8,128)} %refs_5_.1, s32[16,16,1152]{2,1,0:T(8,128)} %refs_6_.1, ...), custom_call_target="tpu_custom_call" | custom-call | tf_op jit(solution)/shard_map/pallas_call | solution.py:579
  41.2 2.1 %shard_map.83 = f32[1,16,16,1152]{3,2,1,0:T(8,128)} custom-call(f32[8,16,1152]{2,1,0:T(8,128)} %get-tuple-element.7.coarse_ref, f32[8,16,1152]{2,1,0:T(8,128)} %get-tuple-element.8.change_ref), custom_call_target="tpu_custom_call" | custom-call | tf_op jit(solution)/shard_map/pallas_call | solution.py:591

commit v6 on v5

--- a/solution.py
+++ b/solution.py
@@ -128,9 +128,9 @@
         )
 
     def send_halo(t, block):
+        ax_copy(t, block).start()
         for copy in ang_copies(t, block):
             copy.start()
-        ax_copy(t, block).start()
 
     def wait_halo(t, block):
         for copy in ang_copies(t, block):
@@ -149,14 +149,6 @@
     def gather(field, face, into):
         for a in range(na):
             into[a : a + 1, :] = field[a, face : face + 1, :]
-
-    @pl.when(chip == 0)
-    def _():
-        pin[...] = jnp.zeros_like(pin)
-
-    @pl.when(chip == chips - 1)
-    def _():
-        sin[...] = jnp.zeros_like(sin)
 
     loads[0].wait()
     sa[0, 0] = u[0, na - 1]
@@ -165,6 +157,14 @@
     pl.semaphore_wait(barrier, len(greet))
     for block in range(len(groups)):
         send_halo(0, block)
+
+    @pl.when(chip == 0)
+    def _():
+        pin[...] = jnp.zeros_like(pin)
+
+    @pl.when(chip == chips - 1)
+    def _():
+        sin[...] = jnp.zeros_like(sin)
 
     loads[1].wait()
     loads[2].wait()
@@ -202,7 +202,6 @@
         gs[i] = mean / (1.0 + own_steps.astype(F32) * rc[i])
         return 0
 
-    lax.fori_loop(0, half, own_factor, 0)
 
     def factors(k, _):
         rate = rc[part * core + k]
@@ -222,7 +221,6 @@
         inv[k] = whole / (whole - 1.0)
         return 0
 
-    lax.fori_loop(0, part, factors, 0)
     for load in loads[3:]:
         load.wait()
 
@@ -412,6 +410,11 @@
         @pl.when(t < STEPS - 1)
         def _():
             by_side(ready)
+
+        @pl.when(t == 0)
+        def _():
+            lax.fori_loop(0, half, own_factor, 0)
+            lax.fori_loop(0, part, factors, 0)
 
         return 0
 

time: 43.5 us -> 43 us (0.989)
  Pallas kernels: 43.3 us -> 42.8 us
    pallas_call x1, Pallas kernels: 41.2 us -> 40.7 us  [local(): pl.pallas_call(functools.partial(kernel, sizes, places, [top.shape[0] for...]
where the time goes in v6:
time: 43 us; the launch traced here: 42.8 us
  Pallas kernels  42.8 us (100%)
    pallas_call x1, Pallas kernels, local(): pl.pallas_call(functools.partial(kernel, sizes, places, [top.shape[0] for...  40.7 us
    pallas_call x1, Pallas kernels, local(): pl.pallas_call(spread, grid=(SPLIT,), out_shape=jax.ShapeDtypeStruct(star...  2.11 us

profile of v6, /device:TPU:0, one launch (start us, length us, event | category | flops | bytes accessed | tf_op | source)
XLA Modules:
  0.0 42.8 jit_solution(258548847503568763)
XLA Ops:
  0.0 40.7 %shard_map.82 = (f32[8,16,1152]{2,1,0:T(8,128)}, f32[8,16,1152]{2,1,0:T(8,128)}) custom-call(s32[8]{0:T(128)} %refs_0_.1, f32[8]{0:T(128)} %refs_1_.1, f32[8]{0:T(128)} %refs_2_.1, f32[8]{0:T(128)} %refs_3_.1, f32[1,16,16,1152]{3,2,1,0:T(8,128)} %refs_4_.1, f32[1,16,16,1152]{3,2,1,0:T(8,128)} %refs_5_.1, s32[16,16,1152]{2,1,0:T(8,128)} %refs_6_.1, ...), custom_call_target="tpu_custom_call" | custom-call | tf_op jit(solution)/shard_map/pallas_call | solution.py:582
  40.7 2.1 %shard_map.83 = f32[1,16,16,1152]{3,2,1,0:T(8,128)} custom-call(f32[8,16,1152]{2,1,0:T(8,128)} %get-tuple-element.7.coarse_ref, f32[8,16,1152]{2,1,0:T(8,128)} %get-tuple-element.8.change_ref), custom_call_target="tpu_custom_call" | custom-call | tf_op jit(solution)/shard_map/pallas_call | solution.py:594

commit v7 on v6

--- a/solution.py
+++ b/solution.py
@@ -86,7 +86,7 @@
     loads = [(s_hbm.at[0], u.at[0]), (ids_hbm, ids_ref), (q_hbm.at[0], q_ref), (w_hbm, w_all)]
     loads = [pltpu.make_async_copy(a, b, in_sem.at[n]) for n, (a, b) in enumerate(loads)]
     barrier = pltpu.get_barrier_semaphore()
-    greet = [("ang", ang, 1, ang_count), ("ang", ang, -1, ang_count)]
+    greet = [("ang", ang, step, ang_count) for step in ((1,) if ang_count == 2 else (1, -1))]
     greet += [("ax", ax, 1, ax_count)]
     greet += [("tm", tm, step, tm_count) for step in (1, -1, 2, -2)]
     for axis, value, step, count in greet:
@@ -153,10 +153,13 @@
     loads[0].wait()
     sa[0, 0] = u[0, na - 1]
     sa[0, 1] = u[0, 0]
-    by_side(lambda face, near: gather(u.at[0], face, sz.at[0]))
     pl.semaphore_wait(barrier, len(greet))
     for block in range(len(groups)):
-        send_halo(0, block)
+        for copy in ang_copies(0, block):
+            copy.start()
+    by_side(lambda face, near: gather(u.at[0], face, sz.at[0]))
+    for block in range(len(groups)):
+        ax_copy(0, block).start()
 
     @pl.when(chip == 0)
     def _():

time: 43 us -> 42.9 us (level)
  no operation moved by 1% of the time
where the time goes in v7:
time: 42.9 us; the launch traced here: 42.7 us
  Pallas kernels  42.7 us (100%)
    pallas_call x1, Pallas kernels, local(): pl.pallas_call(functools.partial(kernel, sizes, places, [top.shape[0] for...  40.6 us
    pallas_call x1, Pallas kernels, local(): pl.pallas_call(spread, grid=(SPLIT,), out_shape=jax.ShapeDtypeStruct(star...  2.11 us

profile of v7, /device:TPU:0, one launch (start us, length us, event | category | flops | bytes accessed | tf_op | source)
XLA Modules:
  0.0 42.7 jit_solution(7244421846405081340)
XLA Ops:
  0.0 40.6 %shard_map.82 = (f32[8,16,1152]{2,1,0:T(8,128)}, f32[8,16,1152]{2,1,0:T(8,128)}) custom-call(s32[8]{0:T(128)} %refs_0_.1, f32[8]{0:T(128)} %refs_1_.1, f32[8]{0:T(128)} %refs_2_.1, f32[8]{0:T(128)} %refs_3_.1, f32[1,16,16,1152]{3,2,1,0:T(8,128)} %refs_4_.1, f32[1,16,16,1152]{3,2,1,0:T(8,128)} %refs_5_.1, s32[16,16,1152]{2,1,0:T(8,128)} %refs_6_.1, ...), custom_call_target="tpu_custom_call" | custom-call | tf_op jit(solution)/shard_map/pallas_call | solution.py:585
  40.6 2.1 %shard_map.83 = f32[1,16,16,1152]{3,2,1,0:T(8,128)} custom-call(f32[8,16,1152]{2,1,0:T(8,128)} %get-tuple-element.7.coarse_ref, f32[8,16,1152]{2,1,0:T(8,128)} %get-tuple-element.8.change_ref), custom_call_target="tpu_custom_call" | custom-call | tf_op jit(solution)/shard_map/pallas_call | solution.py:597
